TPU v7x, 512 devices: a whole 4x4x16 slice. The times are simulated.
512 devices in a mesh: seq: 32 (over z, core), head: 16 (over x, y).
Axes of the slice: x: 4, y: 4, z: 16, core: 2. Of those that a mesh axis runs over, the one named last changes fastest.
Arguments:
- queries: bfloat16 [4096, 16384], P('seq', 'head'), may hold values from -360 to 360, as said below
- keys: bfloat16 [4096, 1024], P('seq', 'head'), may hold values from -6 to 6
- values: bfloat16 [4096, 1024], P('seq', 'head'), may hold values from -6 to 6
- directions: bfloat16 [4096, 1024], P('seq', 'head'), may hold values from -6 to 6
- beta: float32 [4096, 8], P('seq'), may hold values from 0.25 to 2
- gain: float32 [128], replicated, may hold values from 0.25 to 1.75
Outputs:
- attended: bfloat16 [4096, 16384], P('seq', 'head')
Inputs may be any that keep to these rules, and one draw needn't show every extreme that they name: `queries`: queries of order one; some rows may be far larger.
All inputs are finite; a program needn't handle non-finite values.
Results may differ from a plain program's by a relative error of at most 0.04.
Values may be sent and summed in bfloat16 or wider, within the bound.
A program may use at most 64 MiB of HBM per device.

v0:
```python
import jax
import jax.numpy as jnp
from jax import lax
from jax.sharding import PartitionSpec as P

exact_mode = lax.Precision.HIGHEST


def partner(value, axis, bit):
    mask = 2**bit
    pairs = [(source, source ^ mask) for source in range(lax.axis_size(axis))]
    return lax.ppermute(value, axis, pairs)


def shifted(shard, axis, by):
    size = lax.axis_size(axis)
    pairs = [(i, i + by) for i in range(size) if 0 <= i + by < size]
    return lax.ppermute(shard, axis, pairs)


def segment_terms(queries, keys, directions, beta):
    length, head_count, head_width = queries.shape
    raw_dirs = directions.astype(jnp.float32)
    unit_dirs = raw_dirs * lax.rsqrt(jnp.sum(raw_dirs * raw_dirs, axis=1, keepdims=True) + 1e-06)
    positions = jnp.arange(length)
    strict_mask = positions[:, None] > positions[None, :]
    causal_mask = positions[:, None] >= positions[None, :]
    intersections = jnp.where(
        strict_mask, jnp.dot(unit_dirs, unit_dirs.T, precision=exact_mode), 0.0
    )
    identity = jnp.eye(length, dtype=jnp.float32)
    scaled_dirs = beta[:, None] * unit_dirs
    keys_wide = keys.astype(jnp.float32)
    key_reach = jnp.where(strict_mask, jnp.dot(unit_dirs, keys_wide.T, precision=exact_mode), 0.0)
    solution = jax.scipy.linalg.solve_triangular(
        identity + intersections * beta[None, :],
        jnp.concatenate([key_reach, unit_dirs], axis=1),
        lower=True,
        unit_diagonal=True,
    )
    moved_keys = keys_wide - jnp.dot(solution[:, :length].T, scaled_dirs, precision=exact_mode)
    transform = jnp.eye(head_width, dtype=jnp.float32) - jnp.dot(
        unit_dirs.T, beta[:, None] * solution[:, length:], precision=exact_mode
    )
    queries_wide = queries.astype(jnp.float32)
    query_reach = jnp.einsum("te,ihe->thi", unit_dirs, queries_wide, precision=exact_mode)
    query_reach = jnp.where(causal_mask.T[:, None, :], query_reach, 0.0)
    coefficients = jax.scipy.linalg.solve_triangular(
        identity + beta[:, None] * intersections,
        query_reach.reshape(length, head_count * length),
        lower=True,
        trans=1,
        unit_diagonal=True,
    ).reshape(length, head_count, length)
    moved_queries = queries_wide - jnp.einsum(
        "thi,te->ihe", coefficients, scaled_dirs, precision=exact_mode
    )
    plain_scores = jnp.einsum("ihe,je->ihj", queries_wide, keys_wide, precision=exact_mode)
    correction = jnp.einsum(
        "thi,tj->ihj", coefficients, beta[:, None] * key_reach, precision=exact_mode
    )
    local_scores = jnp.where(
        causal_mask[:, None, :], (plain_scores - correction) * head_width ** (-0.5), -1e30
    )
    return (moved_queries, moved_keys, transform, local_scores)


def joined(parity, own_part, other_part, dim):
    first = jnp.concatenate([own_part, other_part], axis=dim)
    second = jnp.concatenate([other_part, own_part], axis=dim)
    return jnp.where(parity == 0, first, second)


def shards(queries, keys, values, directions, beta, gain):
    length = directions.shape[0]
    head_width = directions.shape[1] * 2
    head_count = queries.shape[1] // head_width
    head_place = lax.axis_index("head")
    parity = head_place % 2
    group_index = head_place // 2
    other_keys, other_values, other_dirs = partner((keys, values, directions), "head", 0)
    key_rows = joined(parity, keys, other_keys, 1)
    value_rows = joined(parity, values, other_values, 1)
    dir_rows = joined(parity, directions, other_dirs, 1)
    picker = (jnp.arange(beta.shape[1]) == group_index).astype(jnp.float32)
    beta_rows = jnp.sum(beta * picker[None, :], axis=1)
    moved_queries, moved_keys, transform, local_scores = segment_terms(
        queries.reshape(length, head_count, head_width), key_rows, dir_rows, beta_rows
    )
    query_rows = moved_queries.reshape(length * head_count, head_width).astype(jnp.bfloat16)
    local_flat = local_scores.reshape(length * head_count, length)
    running_max = jnp.max(local_flat, axis=1)
    weights_exp = jnp.exp(local_flat - running_max[:, None])
    running_sum = jnp.sum(weights_exp, axis=1)
    running_out = jnp.dot(
        weights_exp.astype(jnp.bfloat16), value_rows, preferred_element_type=jnp.float32
    )
    key_travel = moved_keys.astype(jnp.bfloat16)
    hop_matrix = transform.astype(jnp.bfloat16)
    segment_index = lax.axis_index("seq")
    scale = head_width ** (-0.5)

    def absorb(stats, key_block, value_block):
        old_max, old_sum, old_out = stats
        scores = jnp.dot(query_rows, key_block.T, preferred_element_type=jnp.float32) * scale
        new_max = jnp.maximum(old_max, jnp.max(scores, axis=1))
        fading = jnp.exp(old_max - new_max)
        block_exp = jnp.exp(scores - new_max[:, None])
        new_sum = old_sum * fading + jnp.sum(block_exp, axis=1)
        new_out = old_out * fading[:, None] + jnp.dot(
            block_exp.astype(jnp.bfloat16), value_block, preferred_element_type=jnp.float32
        )
        return (new_max, new_sum, new_out)

    def forward(key_block):
        return jnp.dot(key_block, hop_matrix.T, preferred_element_type=jnp.float32).astype(
            jnp.bfloat16
        )

    def keep(stats_now):
        return stats_now

    stats = (running_max, running_sum, running_out)

    def advance(step_index, carried):
        key_block, value_block = shifted((carried[0], carried[1]), "seq", 1)

        def take(stats_now):
            return absorb(stats_now, key_block, value_block)

        new_stats = lax.cond(step_index <= segment_index, take, keep, carried[2])
        return (forward(key_block), value_block, new_stats)

    carried = lax.fori_loop(1, lax.axis_size("seq"), advance, (key_travel, value_rows, stats))
    final_max, final_sum, final_out = carried[2]
    mixed = final_out / final_sum[:, None]
    strength = lax.rsqrt(jnp.mean(mixed * mixed, axis=1, keepdims=True) + 1e-06)
    normed = mixed * strength * gain[None, :]
    return normed.reshape(length, head_count * head_width).astype(jnp.bfloat16)


def solution(mesh):
    placed = (
        P("seq", "head"),
        P("seq", "head"),
        P("seq", "head"),
        P("seq", "head"),
        P("seq", None),
        P(),
    )
    return jax.shard_map(
        shards, mesh=mesh, in_specs=placed, out_specs=P("seq", "head"), check_vma=False
    )
```

profile of v0, /device:TPU:384, one launch (start us, length us, event | category | flops | bytes accessed | tf_op | source)
XLA Modules:
  0.0 325.3 jit_solution(10975483945554571445)
XLA Ops:
  0.9 3.6 %collective-permute-start.3 = (bf16[128,64]{1,0:T(8,128)(2,1)S(1)}, bf16[128,64]{1,0:T(8,128)(2,1)S(1)}, u32[]{:S(2)}, u32[]{:S(2)}) collective-permute-start(bf16[128,64]{1,0:T(8,128)(2,1)S(1)} %copy.42), channel_id=1, source_target_pairs={{0,1},{1,0},{2,3},{3,2},{4,5},{5,4},{6,7},{7,6},{8,9},{9,8},{10,11... | collective-permute-start | bytes 49160 | tf_op jit(solution)/shard_map/ppermute | solution.py:12
  7.1 3.5 %collective-permute-start.4 = (bf16[128,64]{1,0:T(8,128)(2,1)S(1)}, bf16[128,64]{1,0:T(8,128)(2,1)S(1)}, u32[]{:S(2)}, u32[]{:S(2)}) collective-permute-start(bf16[128,64]{1,0:T(8,128)(2,1)S(1)} %copy.46), channel_id=1, source_target_pairs={{0,1},{1,0},{2,3},{3,2},{4,5},{5,4},{6,7},{7,6},{8,9},{9,8},{10,11... | collective-permute-start | bytes 49160 | tf_op jit(solution)/shard_map/ppermute | solution.py:12
  13.8 9.8 %custom-call.9 = f32[1,128,128]{1,2,0:T(8,128)S(1)} custom-call(f32[1,128,128]{2,1,0:T(8,128)S(1)} %get-tuple-element.219), custom_call_target="InvertDiagBlocksLowerTriangular" | custom-call | tf_op jit(solution)/shard_map/jit(_solve_triangular)/triangular_solve | solution.py:48
  26.0 9.8 %custom-call.8 = f32[1,128,128]{1,2,0:T(8,128)S(1)} custom-call(f32[1,128,128]{2,1,0:T(8,128)S(1)} %get-tuple-element.220), custom_call_target="InvertDiagBlocksLowerTriangular" | custom-call | tf_op jit(solution)/shard_map/jit(_solve_triangular)/triangular_solve | solution.py:35
  38.9 284.2 %while.21 = (s32[]{:T(128)}, bf16[128,128]{1,0:T(8,128)(2,1)S(1)}, bf16[128,128]{1,0:T(8,128)(2,1)S(1)}, f32[1024]{0:T(1024)S(1)}, f32[1024]{0:T(1024)S(1)}, /*i...) while((s32[]{:T(128)}, bf16[128,128]{1,0:T(8,128)(2,1)S(1)}, ...), condition=%wide.region_9.10_spmd, body=%wide.region_4.9_spmd.sunk | while | flops 72370176 | bytes 3440939 | solution.py:134
  40.8 3.0 collective-permute-start.1
  52.1 2.6 collective-permute-done
  80.1 2.6 collective-permute-done
  89.5 2.6 collective-permute-done
  98.9 2.6 collective-permute-done
  117.6 2.6 collective-permute-done
  126.9 2.6 collective-permute-done
  136.3 2.6 collective-permute-done
  155.0 2.6 collective-permute-done
  164.3 2.6 collective-permute-done
  173.7 2.6 collective-permute-done
  183.1 2.6 collective-permute-done
  220.5 2.6 collective-permute-done
  229.8 2.6 collective-permute-done
  239.2 2.6 collective-permute-done
  257.9 2.6 collective-permute-done
  284.3 2.6 collective-permute-done
  292.8 2.6 collective-permute-done
  309.9 2.6 collective-permute-done
  (391 shorter events, 266.2 us)
Async XLA Ops:
  0.9 11.9 %collective-permute-start.3 = (bf16[128,64]{1,0:T(8,128)(2,1)S(1)}, bf16[128,64]{1,0:T(8,128)(2,1)S(1)}, u32[]{:S(2)}, u32[]{:S(2)}) collective-permute-start(bf16[128,64]{1,0:T(8,128)(2,1)S(1)} %copy.42), channel_id=1, source_target_pairs={{0,1},{1,0},{2,3},{3,2},{4,5},{5,4},{6,7},{7,6},{8,9},{9,8},{10,11... | collective-permute-start | bytes 49160 | tf_op jit(solution)/shard_map/ppermute | solution.py:12
  4.6 20.4 %collective-permute-start.2 = (bf16[128,64]{1,0:T(8,128)(2,1)S(1)}, bf16[128,64]{1,0:T(8,128)(2,1)S(1)}, u32[]{:S(2)}, u32[]{:S(2)}) collective-permute-start(bf16[128,64]{1,0:T(8,128)(2,1)S(1)} %copy.39), channel_id=1, source_target_pairs={{0,1},{1,0},{2,3},{3,2},{4,5},{5,4},{6,7},{7,6},{8,9},{9,8},{10,11... | collective-permute-start | bytes 49160 | tf_op jit(solution)/shard_map/ppermute | solution.py:12
  7.1 31.2 %collective-permute-start.4 = (bf16[128,64]{1,0:T(8,128)(2,1)S(1)}, bf16[128,64]{1,0:T(8,128)(2,1)S(1)}, u32[]{:S(2)}, u32[]{:S(2)}) collective-permute-start(bf16[128,64]{1,0:T(8,128)(2,1)S(1)} %copy.46), channel_id=1, source_target_pairs={{0,1},{1,0},{2,3},{3,2},{4,5},{5,4},{6,7},{7,6},{8,9},{9,8},{10,11... | collective-permute-start | bytes 49160 | tf_op jit(solution)/shard_map/ppermute | solution.py:12
  48.2 6.5 %collective-permute-start = (bf16[128,128]{1,0:T(8,128)(2,1)S(1)}, bf16[128,128]{1,0:T(8,128)(2,1)S(1)}, u32[]{:S(2)}, u32[]{:S(2)}) collective-permute-start(bf16[128,128]{1,0:T(8,128)(2,1)S(1)} %get-tuple-element.301), channel_id=1, source_target_pairs={{0,16},{16,32},{32,48},{48,64},{64,80},{80,96},{96,112},{112,128},... | collective-permute-start | bytes 98312 | tf_op jit(solution)/shard_map/while/body/eval_jaxpr/ppermute | solution.py:18
  57.6 6.5 %collective-permute-start = (bf16[128,128]{1,0:T(8,128)(2,1)S(1)}, bf16[128,128]{1,0:T(8,128)(2,1)S(1)}, u32[]{:S(2)}, u32[]{:S(2)}) collective-permute-start(bf16[128,128]{1,0:T(8,128)(2,1)S(1)} %get-tuple-element.301), channel_id=1, source_target_pairs={{0,16},{16,32},{32,48},{48,64},{64,80},{80,96},{96,112},{112,128},... | collective-permute-start | bytes 98312 | tf_op jit(solution)/shard_map/while/body/eval_jaxpr/ppermute | solution.py:18
  66.9 6.5 %collective-permute-start = (bf16[128,128]{1,0:T(8,128)(2,1)S(1)}, bf16[128,128]{1,0:T(8,128)(2,1)S(1)}, u32[]{:S(2)}, u32[]{:S(2)}) collective-permute-start(bf16[128,128]{1,0:T(8,128)(2,1)S(1)} %get-tuple-element.301), channel_id=1, source_target_pairs={{0,16},{16,32},{32,48},{48,64},{64,80},{80,96},{96,112},{112,128},... | collective-permute-start | bytes 98312 | tf_op jit(solution)/shard_map/while/body/eval_jaxpr/ppermute | solution.py:18
  76.3 6.5 %collective-permute-start = (bf16[128,128]{1,0:T(8,128)(2,1)S(1)}, bf16[128,128]{1,0:T(8,128)(2,1)S(1)}, u32[]{:S(2)}, u32[]{:S(2)}) collective-permute-start(bf16[128,128]{1,0:T(8,128)(2,1)S(1)} %get-tuple-element.301), channel_id=1, source_target_pairs={{0,16},{16,32},{32,48},{48,64},{64,80},{80,96},{96,112},{112,128},... | collective-permute-start | bytes 98312 | tf_op jit(solution)/shard_map/while/body/eval_jaxpr/ppermute | solution.py:18
  85.6 6.5 %collective-permute-start = (bf16[128,128]{1,0:T(8,128)(2,1)S(1)}, bf16[128,128]{1,0:T(8,128)(2,1)S(1)}, u32[]{:S(2)}, u32[]{:S(2)}) collective-permute-start(bf16[128,128]{1,0:T(8,128)(2,1)S(1)} %get-tuple-element.301), channel_id=1, source_target_pairs={{0,16},{16,32},{32,48},{48,64},{64,80},{80,96},{96,112},{112,128},... | collective-permute-start | bytes 98312 | tf_op jit(solution)/shard_map/while/body/eval_jaxpr/ppermute | solution.py:18
  95.0 6.5 %collective-permute-start = (bf16[128,128]{1,0:T(8,128)(2,1)S(1)}, bf16[128,128]{1,0:T(8,128)(2,1)S(1)}, u32[]{:S(2)}, u32[]{:S(2)}) collective-permute-start(bf16[128,128]{1,0:T(8,128)(2,1)S(1)} %get-tuple-element.301), channel_id=1, source_target_pairs={{0,16},{16,32},{32,48},{48,64},{64,80},{80,96},{96,112},{112,128},... | collective-permute-start | bytes 98312 | tf_op jit(solution)/shard_map/while/body/eval_jaxpr/ppermute | solution.py:18
  104.3 6.5 %collective-permute-start = (bf16[128,128]{1,0:T(8,128)(2,1)S(1)}, bf16[128,128]{1,0:T(8,128)(2,1)S(1)}, u32[]{:S(2)}, u32[]{:S(2)}) collective-permute-start(bf16[128,128]{1,0:T(8,128)(2,1)S(1)} %get-tuple-element.301), channel_id=1, source_target_pairs={{0,16},{16,32},{32,48},{48,64},{64,80},{80,96},{96,112},{112,128},... | collective-permute-start | bytes 98312 | tf_op jit(solution)/shard_map/while/body/eval_jaxpr/ppermute | solution.py:18
  113.7 6.5 %collective-permute-start = (bf16[128,128]{1,0:T(8,128)(2,1)S(1)}, bf16[128,128]{1,0:T(8,128)(2,1)S(1)}, u32[]{:S(2)}, u32[]{:S(2)}) collective-permute-start(bf16[128,128]{1,0:T(8,128)(2,1)S(1)} %get-tuple-element.301), channel_id=1, source_target_pairs={{0,16},{16,32},{32,48},{48,64},{64,80},{80,96},{96,112},{112,128},... | collective-permute-start | bytes 98312 | tf_op jit(solution)/shard_map/while/body/eval_jaxpr/ppermute | solution.py:18
  123.0 6.5 %collective-permute-start = (bf16[128,128]{1,0:T(8,128)(2,1)S(1)}, bf16[128,128]{1,0:T(8,128)(2,1)S(1)}, u32[]{:S(2)}, u32[]{:S(2)}) collective-permute-start(bf16[128,128]{1,0:T(8,128)(2,1)S(1)} %get-tuple-element.301), channel_id=1, source_target_pairs={{0,16},{16,32},{32,48},{48,64},{64,80},{80,96},{96,112},{112,128},... | collective-permute-start | bytes 98312 | tf_op jit(solution)/shard_map/while/body/eval_jaxpr/ppermute | solution.py:18
  132.4 6.5 %collective-permute-start = (bf16[128,128]{1,0:T(8,128)(2,1)S(1)}, bf16[128,128]{1,0:T(8,128)(2,1)S(1)}, u32[]{:S(2)}, u32[]{:S(2)}) collective-permute-start(bf16[128,128]{1,0:T(8,128)(2,1)S(1)} %get-tuple-element.301), channel_id=1, source_target_pairs={{0,16},{16,32},{32,48},{48,64},{64,80},{80,96},{96,112},{112,128},... | collective-permute-start | bytes 98312 | tf_op jit(solution)/shard_map/while/body/eval_jaxpr/ppermute | solution.py:18
  141.8 6.5 %collective-permute-start = (bf16[128,128]{1,0:T(8,128)(2,1)S(1)}, bf16[128,128]{1,0:T(8,128)(2,1)S(1)}, u32[]{:S(2)}, u32[]{:S(2)}) collective-permute-start(bf16[128,128]{1,0:T(8,128)(2,1)S(1)} %get-tuple-element.301), channel_id=1, source_target_pairs={{0,16},{16,32},{32,48},{48,64},{64,80},{80,96},{96,112},{112,128},... | collective-permute-start | bytes 98312 | tf_op jit(solution)/shard_map/while/body/eval_jaxpr/ppermute | solution.py:18
  151.1 6.5 %collective-permute-start = (bf16[128,128]{1,0:T(8,128)(2,1)S(1)}, bf16[128,128]{1,0:T(8,128)(2,1)S(1)}, u32[]{:S(2)}, u32[]{:S(2)}) collective-permute-start(bf16[128,128]{1,0:T(8,128)(2,1)S(1)} %get-tuple-element.301), channel_id=1, source_target_pairs={{0,16},{16,32},{32,48},{48,64},{64,80},{80,96},{96,112},{112,128},... | collective-permute-start | bytes 98312 | tf_op jit(solution)/shard_map/while/body/eval_jaxpr/ppermute | solution.py:18
  160.5 6.5 %collective-permute-start = (bf16[128,128]{1,0:T(8,128)(2,1)S(1)}, bf16[128,128]{1,0:T(8,128)(2,1)S(1)}, u32[]{:S(2)}, u32[]{:S(2)}) collective-permute-start(bf16[128,128]{1,0:T(8,128)(2,1)S(1)} %get-tuple-element.301), channel_id=1, source_target_pairs={{0,16},{16,32},{32,48},{48,64},{64,80},{80,96},{96,112},{112,128},... | collective-permute-start | bytes 98312 | tf_op jit(solution)/shard_map/while/body/eval_jaxpr/ppermute | solution.py:18
  169.8 6.5 %collective-permute-start = (bf16[128,128]{1,0:T(8,128)(2,1)S(1)}, bf16[128,128]{1,0:T(8,128)(2,1)S(1)}, u32[]{:S(2)}, u32[]{:S(2)}) collective-permute-start(bf16[128,128]{1,0:T(8,128)(2,1)S(1)} %get-tuple-element.301), channel_id=1, source_target_pairs={{0,16},{16,32},{32,48},{48,64},{64,80},{80,96},{96,112},{112,128},... | collective-permute-start | bytes 98312 | tf_op jit(solution)/shard_map/while/body/eval_jaxpr/ppermute | solution.py:18
  179.2 6.5 %collective-permute-start = (bf16[128,128]{1,0:T(8,128)(2,1)S(1)}, bf16[128,128]{1,0:T(8,128)(2,1)S(1)}, u32[]{:S(2)}, u32[]{:S(2)}) collective-permute-start(bf16[128,128]{1,0:T(8,128)(2,1)S(1)} %get-tuple-element.301), channel_id=1, source_target_pairs={{0,16},{16,32},{32,48},{48,64},{64,80},{80,96},{96,112},{112,128},... | collective-permute-start | bytes 98312 | tf_op jit(solution)/shard_map/while/body/eval_jaxpr/ppermute | solution.py:18
  188.5 6.5 %collective-permute-start = (bf16[128,128]{1,0:T(8,128)(2,1)S(1)}, bf16[128,128]{1,0:T(8,128)(2,1)S(1)}, u32[]{:S(2)}, u32[]{:S(2)}) collective-permute-start(bf16[128,128]{1,0:T(8,128)(2,1)S(1)} %get-tuple-element.301), channel_id=1, source_target_pairs={{0,16},{16,32},{32,48},{48,64},{64,80},{80,96},{96,112},{112,128},... | collective-permute-start | bytes 98312 | tf_op jit(solution)/shard_map/while/body/eval_jaxpr/ppermute | solution.py:18
  197.9 6.5 %collective-permute-start = (bf16[128,128]{1,0:T(8,128)(2,1)S(1)}, bf16[128,128]{1,0:T(8,128)(2,1)S(1)}, u32[]{:S(2)}, u32[]{:S(2)}) collective-permute-start(bf16[128,128]{1,0:T(8,128)(2,1)S(1)} %get-tuple-element.301), channel_id=1, source_target_pairs={{0,16},{16,32},{32,48},{48,64},{64,80},{80,96},{96,112},{112,128},... | collective-permute-start | bytes 98312 | tf_op jit(solution)/shard_map/while/body/eval_jaxpr/ppermute | solution.py:18
  207.2 6.5 %collective-permute-start = (bf16[128,128]{1,0:T(8,128)(2,1)S(1)}, bf16[128,128]{1,0:T(8,128)(2,1)S(1)}, u32[]{:S(2)}, u32[]{:S(2)}) collective-permute-start(bf16[128,128]{1,0:T(8,128)(2,1)S(1)} %get-tuple-element.301), channel_id=1, source_target_pairs={{0,16},{16,32},{32,48},{48,64},{64,80},{80,96},{96,112},{112,128},... | collective-permute-start | bytes 98312 | tf_op jit(solution)/shard_map/while/body/eval_jaxpr/ppermute | solution.py:18
  226.0 6.5 %collective-permute-start = (bf16[128,128]{1,0:T(8,128)(2,1)S(1)}, bf16[128,128]{1,0:T(8,128)(2,1)S(1)}, u32[]{:S(2)}, u32[]{:S(2)}) collective-permute-start(bf16[128,128]{1,0:T(8,128)(2,1)S(1)} %get-tuple-element.301), channel_id=1, source_target_pairs={{0,16},{16,32},{32,48},{48,64},{64,80},{80,96},{96,112},{112,128},... | collective-permute-start | bytes 98312 | tf_op jit(solution)/shard_map/while/body/eval_jaxpr/ppermute | solution.py:18
  280.4 6.5 %collective-permute-start = (bf16[128,128]{1,0:T(8,128)(2,1)S(1)}, bf16[128,128]{1,0:T(8,128)(2,1)S(1)}, u32[]{:S(2)}, u32[]{:S(2)}) collective-permute-start(bf16[128,128]{1,0:T(8,128)(2,1)S(1)} %get-tuple-element.301), channel_id=1, source_target_pairs={{0,16},{16,32},{32,48},{48,64},{64,80},{80,96},{96,112},{112,128},... | collective-permute-start | bytes 98312 | tf_op jit(solution)/shard_map/while/body/eval_jaxpr/ppermute | solution.py:18
  306.0 6.5 %collective-permute-start = (bf16[128,128]{1,0:T(8,128)(2,1)S(1)}, bf16[128,128]{1,0:T(8,128)(2,1)S(1)}, u32[]{:S(2)}, u32[]{:S(2)}) collective-permute-start(bf16[128,128]{1,0:T(8,128)(2,1)S(1)} %get-tuple-element.301), channel_id=1, source_target_pairs={{0,16},{16,32},{32,48},{48,64},{64,80},{80,96},{96,112},{112,128},... | collective-permute-start | bytes 98312 | tf_op jit(solution)/shard_map/while/body/eval_jaxpr/ppermute | solution.py:18
  (45 other events, 276.3 us)
where the time goes:
time: 327 us; the launch traced here: 325 us
  waiting for transfers between devices  139 us (43%)
  starting transfers between devices  130 us (40%)
  matrix products  24.8 us (8%)
  other arithmetic  23.9 us (7%)
  local copies, waits for them, and re-layouts  5.23 us (2%)
    ppermute x62, waiting for transfers between devices, shifted(): return lax.ppermute(shard, axis, pairs)  139 us
    ppermute x62, starting transfers between devices, shifted(): return lax.ppermute(shard, axis, pairs)  121 us
    dot_general x24, matrix products, absorb(): jnp.dot(block_exp.astype(jnp.bfloat16), value_block, preferred_element_ty...  10.4 us
    another operation x2, other arithmetic, segment_terms(): jax.scipy.linalg.solve_triangular(identity + intersections * beta[None, :...  9.81 us
    another operation x1, other arithmetic, segment_terms(): jax.scipy.linalg.solve_triangular(identity + beta[:, None] * intersection...  9.81 us
    ppermute x3, starting transfers between devices, partner(): return lax.ppermute(value, axis, pairs)  9.46 us
  transfers between devices with their start and end apart: 65, of which 62 were waited for; matrix products, arithmetic and copies ran while one was open for 8% of the time, Pallas kernels for 0%

commit v1 on v0

v1 whole, which is shorter than its diff:
```python
import functools
import math

import jax
import jax.numpy as jnp
from jax import lax
from jax.experimental import pallas as pl
from jax.experimental.pallas import tpu as pltpu
from jax.sharding import PartitionSpec as P

MESH = pl.DeviceIdType.MESH
F32 = jnp.float32
BF16 = jnp.bfloat16
NN = (((1,), (0,)), ((), ()))
NT = (((1,), (1,)), ((), ()))
LOW = -1e30
KW, VAL = 0, 1


def mm(a, b, dims=NN):
    return lax.dot_general(a, b, dims, preferred_element_type=F32)


def split(x):
    high = x.astype(BF16)
    return high, (x - high.astype(F32)).astype(BF16)


def mm3(a, b, dims=NN):
    return mm(a[0], b[0], dims) + (mm(a[0], b[1], dims) + mm(a[1], b[0], dims))


def kernel(
    chips, q_ref, k_ref, v_ref, u_ref, beta_ref, gain_ref, o_ref,
    got_u, got_k, got_v, own_seg, sib_seg, kw, val, q_rows, peak, total, acc, chain, keys_now,
    pair_send, pair_recv, line_send, line_recv, near_send, near_recv, ready,
):
    tokens, width = k_ref.shape[0], 2 * k_ref.shape[1]
    heads = q_ref.shape[1] // width
    half = width // 2
    factor = math.log2(math.e) / math.sqrt(width)
    s, h = lax.axis_index("seq"), lax.axis_index("head")
    z, c = lax.div(s, 2), lax.rem(s, 2)
    last = chips - 1

    def chip(place):
        return (place * 2 + c, h)

    partner = (s, h + 1 - 2 * lax.rem(h, 2))
    sibling = (s + 1 - 2 * c, h)

    barrier = pltpu.get_barrier_semaphore()

    def tell(sem, device):
        pl.semaphore_signal(sem, inc=1, device_id=device, device_id_type=MESH)

    tell(barrier, partner)
    tell(barrier, sibling)
    pl.when(z + 1 <= last)(lambda: tell(barrier, chip(z + 1)))
    pl.when(z + 2 <= last)(lambda: tell(barrier, chip(z + 2)))
    pl.when(z <= 1)(lambda: tell(barrier, chip(last)))
    pl.when(z == 0)(lambda: tell(barrier, chip(last - 1)))
    extra = jnp.where(z == last, 2, jnp.where(z == last - 1, 1, 0))
    pl.semaphore_wait(barrier, 2 + jnp.minimum(z, 2) + extra)
    pl.when(z >= 1)(lambda: tell(ready.at[0], chip(z - 1)))
    pl.when(z >= 2)(lambda: tell(ready.at[1], chip(z - 2)))
    pl.when(z == last)(lambda: tell(ready.at[2], chip(0)))
    pl.when(z == last)(lambda: tell(ready.at[3], chip(1)))
    pl.when(z == last - 1)(lambda: tell(ready.at[3], chip(0)))

    swaps = [
        pltpu.make_async_remote_copy(
            src, dst, pair_send.at[i], pair_recv.at[i], device_id=partner, device_id_type=MESH
        )
        for i, (src, dst) in enumerate(((u_ref, got_u), (k_ref, got_k), (v_ref, got_v)))
    ]
    for copy in swaps:
        copy.start()
    even = lax.rem(h, 2) == 0

    def joined(own, other):
        own, other = own[...].astype(F32), other[...].astype(F32)
        return jnp.where(
            even, jnp.concatenate([own, other], axis=1), jnp.concatenate([other, own], axis=1)
        )

    rows_i = lax.broadcasted_iota(jnp.int32, (tokens, tokens), 0)
    cols_i = lax.broadcasted_iota(jnp.int32, (tokens, tokens), 1)
    eye = (rows_i == cols_i).astype(F32)
    lane = lax.broadcasted_iota(jnp.int32, beta_ref.shape, 1)
    beta = jnp.sum(jnp.where(lane == lax.div(h, 2), beta_ref[...], 0.0), axis=1, keepdims=True)

    buffers = (kw, val)

    def line_copy(kind, source_slot, target_slot, device):
        return pltpu.make_async_remote_copy(
            buffers[kind].at[source_slot, c],
            buffers[kind].at[target_slot, c],
            line_send.at[kind, target_slot],
            line_recv.at[kind, target_slot],
            device_id=device,
            device_id_type=MESH,
        )

    def near_copy(kind, slot):
        return pltpu.make_async_remote_copy(
            buffers[kind].at[slot, c],
            buffers[kind].at[slot, c],
            near_send.at[kind, slot],
            near_recv.at[kind, slot],
            device_id=sibling,
            device_id_type=MESH,
        )

    def near_arrival(kind, slot):
        return pltpu.make_async_remote_copy(
            buffers[kind].at[slot, 1 - c],
            buffers[kind].at[slot, 1 - c],
            near_send.at[kind, slot],
            near_recv.at[kind, slot],
            device_id=sibling,
            device_id_type=MESH,
        )

    reach = chips // 2
    far = chips - reach - 1

    def forward_relays(kind, d, act):
        @pl.when((z >= d) & (d + 1 <= reach) & (z + 1 <= last))
        def _():
            act(line_copy(kind, d, d + 1, chip(z + 1)))

        @pl.when((z >= d) & (d + 2 <= reach) & (z + 2 <= last))
        def _():
            act(line_copy(kind, d, d + 2, chip(z + 2)))

    def backward_relays(kind, e, act):
        slot = lax.rem(chips - e, chips) if not isinstance(e, int) else (chips - e) % chips
        wrapped = z + e >= chips
        held = (z + e < far) | wrapped

        @pl.when(held & (wrapped | (z == 0)) & (e + 1 <= far))
        def _():
            act(line_copy(kind, slot, chips - e - 1, chip(lax.rem(z + chips - 1, chips))))

        @pl.when(held & (e + 2 < far))
        def _():
            act(line_copy(kind, slot, chips - e - 2, chip(lax.rem(z + chips - 2, chips))))

    def begin(copy):
        copy.start()

    def arrive(kind, slot):
        line_copy(kind, slot, slot, sibling).wait_recv()

    def receive(kind, m):
        d1, d2 = 2 * m + 1, 2 * m + 2

        @pl.when(z >= d2)
        def _():
            arrive(kind, d2)

        forward_relays(kind, d2, begin)
        pl.when(z >= d2)(lambda: near_copy(kind, d2).start())

        @pl.when((d2 < far) & ((z + d2 < far) | (z + d2 >= chips)))
        def _():
            arrive(kind, chips - d2)

        @pl.when(d2 < far)
        def _():
            backward_relays(kind, d2, begin)

        @pl.when(z >= d1)
        def _():
            arrive(kind, d1)
            near_copy(kind, d1).start()

        @pl.when((d2 < far) & (z + d2 >= chips))
        def _():
            near_copy(kind, chips - d2).start()

        @pl.when((d1 <= far) & (z + d1 >= chips))
        def _():
            arrive(kind, chips - d1)
            near_copy(kind, chips - d1).start()

    swaps[0].wait_recv()
    raw = joined(u_ref, got_u)
    unit = raw * lax.rsqrt(jnp.sum(raw * raw, axis=1, keepdims=True) + 1e-06)
    scaled = beta * unit
    unit2, scaled2 = split(unit), split(scaled)
    nil = jnp.where(rows_i > cols_i, mm3(scaled2, unit2, NT), 0.0)
    swaps[1].wait_recv()
    keys_wide = joined(k_ref, got_k)
    keys_own = keys_wide.astype(BF16)
    reach_t = jnp.where(
        cols_i > rows_i, mm(keys_own, scaled2[0], NT) + mm(keys_own, scaled2[1], NT), 0.0
    )
    swaps[2].wait_recv()
    val[0, pl.ds(c, 1)] = joined(v_ref, got_v).astype(BF16)[None]
    near_copy(VAL, 0).start()

    @pl.when(lax.rem(z, 2) == 1)
    def _():
        kw[pl.ds(z + 1, 1)] = jnp.zeros((1,) + kw.shape[1:], BF16)
        val[pl.ds(z + 1, 1)] = jnp.zeros((1,) + val.shape[1:], BF16)

    pl.when(z + 1 <= last)(lambda: pl.semaphore_wait(ready.at[0], 1))
    pl.when(z + 2 <= last)(lambda: pl.semaphore_wait(ready.at[1], 1))
    forward_relays(VAL, 0, begin)

    inverse = eye
    size = 1
    while size < tokens:
        bits = size.bit_length() - 1
        block_r, block_c = rows_i >> bits, cols_i >> bits
        corner = jnp.where(((block_r & 1) == 1) & (block_c == block_r - 1), nil, 0.0)
        if size == 1:
            inverse = eye - corner
        else:
            inv2 = split(inverse)
            inverse = inverse - mm3(split(mm3(inv2, split(corner))), inv2)
        size *= 2
    solved2 = split(
        mm3(split(jnp.concatenate([jnp.transpose(scaled), reach_t], axis=0)), split(inverse), NT)
    )
    ends = jnp.concatenate([eye, keys_wide], axis=0) - mm3(solved2, unit2)
    own_seg[...] = ends.astype(BF16)

    seg_swap = pltpu.make_async_remote_copy(
        own_seg, sib_seg, pair_send.at[3], pair_recv.at[3], device_id=sibling, device_id_type=MESH
    )
    seg_swap.start()
    seg_swap.wait_recv()
    first = c == 0
    own_hop, own_keys = own_seg[0:width, :], own_seg[width : width + tokens, :]
    sib_hop, sib_keys = sib_seg[0:width, :], sib_seg[width : width + tokens, :]
    moved = jnp.where(first, mm(own_keys, sib_hop), own_keys.astype(F32))
    hops = jnp.where(first, mm(own_hop, sib_hop), mm(sib_hop, own_hop))
    hops = jnp.where(first, hops[0:half, :], hops[half:, :])
    kw[0, pl.ds(c, 1)] = jnp.concatenate([moved, hops], axis=0).astype(BF16)[None]
    forward_relays(KW, 0, begin)

    pl.when(z <= 1)(lambda: pl.semaphore_wait(ready.at[3], 1))
    pl.when(z == 0)(lambda: pl.semaphore_wait(ready.at[2], 1))
    backward_relays(VAL, 0, begin)
    backward_relays(KW, 0, begin)

    values_own = val[0, pl.ds(c, 1)].reshape(tokens, width)
    sides = jnp.concatenate([unit2[0], unit2[1], keys_own], axis=0)
    for head in range(heads):
        span = slice(head * tokens, (head + 1) * tokens)
        q = q_ref[:, head * width : (head + 1) * width]
        products = mm(q, sides, NT)
        onto = products[:, 0:tokens] + products[:, tokens : 2 * tokens]
        onto2 = split(jnp.where(rows_i >= cols_i, onto, 0.0))
        taken = mm3(onto2, solved2, NT)
        q_rows[span, :] = (q.astype(F32) - taken[:, 0:width]).astype(BF16)
        scores = (products[:, 2 * tokens :] - taken[:, width:]) * factor
        scores = jnp.where(rows_i >= cols_i, scores, LOW)
        top = jnp.max(scores, axis=1, keepdims=True)
        weights = jnp.exp2(scores - top)
        peak[span, :] = jnp.broadcast_to(top, (tokens, width))
        total[span, :] = weights
        acc[span, :] = mm(weights.astype(BF16), values_own)

    def absorb(key_block, value_block, mask):
        for head in range(heads):
            span = slice(head * tokens, (head + 1) * tokens)
            scores = mask(mm(q_rows[span, :], key_block(), NT))
            old = peak[span, :]
            top = jnp.maximum(old, jnp.max(scores, axis=1, keepdims=True))
            fade = jnp.exp2(old - top)
            peak[span, :] = top
            parts = []
            sums = total[span, :] * fade
            for i in range(scores.shape[1] // width):
                weights = jnp.exp2(scores[:, i * width : (i + 1) * width] - top)
                sums = sums + weights
                parts.append(weights.astype(BF16))
            total[span, :] = sums
            both = jnp.concatenate(parts, axis=1) if len(parts) > 1 else parts[0]
            acc[span, :] = acc[span, :] * fade + mm(both, value_block())

    near_arrival(VAL, 0).wait_recv()

    @pl.when(c == 1)
    def _():
        keys_now[0:tokens, :] = (sib_seg[width : width + tokens, :].astype(F32) * factor).astype(BF16)
        absorb(lambda: keys_now[0:tokens, :], lambda: val[0, 0], lambda x: x)

    chain[...] = jnp.where(first, eye, sib_seg[0:width, :].astype(F32)).astype(BF16)
    receive(VAL, 0)

    @pl.loop(0, (chips + 1) // 2)
    def _(m):
        @pl.when(2 * m < reach)
        def _():
            receive(KW, m)

        @pl.when(2 * m + 2 < reach)
        def _():
            receive(VAL, m + 1)

        @pl.when(z >= 2 * m + 1)
        def _():
            d1, d2 = 2 * m + 1, 2 * m + 2
            for kind in (KW, VAL):
                near_arrival(kind, d1).wait_recv()
                pl.when(z >= d2)(lambda kind=kind: near_arrival(kind, d2).wait_recv())
            for i, d in enumerate((d1, d2)):
                now = chain[...]
                for core in range(2):
                    block = mm(kw[d, core, 0:tokens, :], now) * factor
                    at = (2 * i + core) * tokens
                    keys_now[at : at + tokens, :] = block.astype(BF16)
                hop = jnp.concatenate(
                    [kw[d, 0, tokens : tokens + half, :], kw[d, 1, tokens : tokens + half, :]], axis=0
                )
                chain[...] = mm(hop, now).astype(BF16)
            both = z >= d2

            def mask(scores):
                n = 2 * tokens
                return jnp.concatenate(
                    [scores[:, 0:n], jnp.where(both, scores[:, n:], LOW)], axis=1
                )

            absorb(
                lambda: keys_now[...],
                lambda: val[pl.ds(d1, 2)].reshape(4 * tokens, width),
                mask,
            )

    gain = gain_ref[...]
    for head in range(heads):
        span = slice(head * tokens, (head + 1) * tokens)
        mixed = acc[span, :] / jnp.sum(total[span, :], axis=1, keepdims=True)
        strength = lax.rsqrt(jnp.mean(mixed * mixed, axis=1, keepdims=True) + 1e-06)
        o_ref[:, head * width : (head + 1) * width] = (mixed * strength * gain).astype(BF16)

    def left(copy):
        copy.wait_send()

    for copy in swaps:
        copy.wait_send()
    seg_swap.wait_send()
    near_copy(VAL, 0).wait_send()

    @pl.loop(0, reach // 2)
    def _(m):
        for kind in (KW, VAL):
            forward_relays(kind, 2 * m, left)

            @pl.when(2 * m < far)
            def _(kind=kind):
                backward_relays(kind, 2 * m, left)

    @pl.loop(1, chips)
    def _(d):
        for kind in (KW, VAL):
            pl.when(z >= d)(lambda kind=kind: near_copy(kind, d).wait_send())


def solution(mesh):
    chips = mesh.shape["seq"] // 2

    def step(q, k, v, u, beta, gain):
        tokens, width = k.shape[0], 2 * k.shape[1]
        rows = tokens * (q.shape[1] // width)
        slots = chips + 1
        vmem = pl.BlockSpec(memory_space=pltpu.VMEM)
        piece = tokens + width // 2
        return pl.pallas_call(
            functools.partial(kernel, chips),
            out_shape=jax.ShapeDtypeStruct(q.shape, BF16),
            in_specs=[vmem] * 6,
            out_specs=vmem,
            scratch_shapes=[
                pltpu.VMEM(k.shape, BF16),
                pltpu.VMEM(k.shape, BF16),
                pltpu.VMEM(k.shape, BF16),
                pltpu.VMEM((width + tokens, width), BF16),
                pltpu.VMEM((width + tokens, width), BF16),
                pltpu.VMEM((slots, 2, piece, width), BF16),
                pltpu.VMEM((slots, 2, tokens, width), BF16),
                pltpu.VMEM((rows, width), BF16),
                pltpu.VMEM((rows, width), F32),
                pltpu.VMEM((rows, width), F32),
                pltpu.VMEM((rows, width), F32),
                pltpu.VMEM((width, width), BF16),
                pltpu.VMEM((4 * tokens, width), BF16),
                pltpu.SemaphoreType.DMA((4,)),
                pltpu.SemaphoreType.DMA((4,)),
                pltpu.SemaphoreType.DMA((2, slots)),
                pltpu.SemaphoreType.DMA((2, slots)),
                pltpu.SemaphoreType.DMA((2, slots)),
                pltpu.SemaphoreType.DMA((2, slots)),
                pltpu.SemaphoreType.REGULAR((4,)),
            ],
            compiler_params=pltpu.CompilerParams(
                collective_id=0, has_side_effects=True, vmem_limit_bytes=40 * 2**20
            ),
        )(q, k, v, u, beta, gain.reshape(1, width))

    return jax.shard_map(
        step,
        mesh=mesh,
        in_specs=(P("seq", "head"),) * 4 + (P("seq", None), P()),
        out_specs=P("seq", "head"),
        check_vma=False,
    )
```

time: 327 us -> 54.7 us (0.17)
  the two profiles are of different devices: /device:TPU:384 before, /device:TPU:485 now
where the time goes in v1:
time: 54.7 us; the launch traced here: 54.4 us
  Pallas kernels  49.8 us (91%)
  local copies, waits for them, and re-layouts  4.54 us (8%)
    pallas_call x1, Pallas kernels, step(): pl.pallas_call(functools.partial(kernel, chips), out_shape=jax.ShapeDtype...  49.8 us
    unnamed x15, local copies, waits for them, and re-layouts  4.54 us

profile of v1, /device:TPU:485, one launch (start us, length us, event | category | flops | bytes accessed | tf_op | source)
XLA Modules:
  0.0 54.4 jit_solution(2872157334574588059)
XLA Ops:
  0.0 0.0 copy-start.2
  0.0 0.8 %copy.7.k_ref = bf16[128,64]{1,0:T(8,128)(2,1)S(1)} copy(bf16[128,64]{0,1:T(8,128)(2,1)} %param.7) | data formatting | bytes 32768 | tf_op args[1]
  0.8 0.0 copy-done.2
  0.9 0.0 copy-start.3
  0.9 0.1 copy.8.v_ref
  1.0 0.6 %copy-done.3 = bf16[128,64]{0,1:T(8,128)(2,1)S(1)} copy-done((bf16[128,64]{0,1:T(8,128)(2,1)S(1)}, bf16[128,64]{0,1:T(8,128)(2,1)}, u32[]{:S(2)}) %copy-start.3) | copy-done | bytes 16408
  1.6 0.0 copy-start.4
  1.6 0.1 copy.9.u_ref
  1.7 0.6 %copy-done.4 = f32[128,8]{0,1:T(8,128)S(1)} copy-done((f32[128,8]{0,1:T(8,128)S(1)}, f32[128,8]{0,1:T(8,128)}, u32[]{:S(2)}) %copy-start.4) | copy-done | bytes 4120
  2.3 0.0 copy-start.1
  2.3 0.1 copy.10.beta_ref
  2.4 0.6 %copy-done.1 = f32[128]{0:T(128)S(1)} copy-done((f32[128]{0:T(128)S(1)}, f32[128]{0:T(128)}, u32[]{:S(2)}) %copy-start.1) | copy-done | bytes 536
  2.9 0.0 copy-start
  2.9 0.9 %copy-done = bf16[128,1024]{1,0:T(8,128)(2,1)S(1)} copy-done((bf16[128,1024]{1,0:T(8,128)(2,1)S(1)}, bf16[128,1024]{1,0:T(8,128)(2,1)}, u32[]{:S(2)}) %copy-start) | copy-done | bytes 262168
  3.9 49.8 %shard_map.64 = bf16[128,1024]{1,0:T(8,128)(2,1)S(1)} custom-call(bf16[128,1024]{1,0:T(8,128)(2,1)S(1)} %copy-done, bf16[128,64]{1,0:T(8,128)(2,1)S(1)} %copy.7.k_ref, bf16[128,64]{1,0:T(8,128)(2,1)S(1)} %copy.8.v_ref, bf16[128,64]{1,0:T(8,128)(2,1)S(1)} %copy.9.u_ref, f32[128,8]{1,0:T(8,128)S(1)} %copy.10.beta_ref, f32[1,128]{1,0:T(1,128)S(1)} %bitcast.1), custom_call_target="tpu_custom_call" | custom-call | tf_op jit(solution)/shard_map/pallas_call | solution.py:375
  53.7 0.7 %copy.12 = bf16[128,1024]{1,0:T(8,128)(2,1)} copy(bf16[128,1024]{1,0:T(8,128)(2,1)S(1)} %shard_map.64) | data formatting | bytes 524288
Async XLA Ops:
  0.0 0.8 %copy-start.2 = (bf16[128,64]{0,1:T(8,128)(2,1)S(1)}, bf16[128,64]{0,1:T(8,128)(2,1)}, u32[]{:S(2)}) copy-start(bf16[128,64]{0,1:T(8,128)(2,1)} %param.8) | copy-start | bytes 49156
  0.9 0.7 %copy-start.3 = (bf16[128,64]{0,1:T(8,128)(2,1)S(1)}, bf16[128,64]{0,1:T(8,128)(2,1)}, u32[]{:S(2)}) copy-start(bf16[128,64]{0,1:T(8,128)(2,1)} %param.9) | copy-start | bytes 49156
  1.6 0.7 %copy-start.4 = (f32[128,8]{0,1:T(8,128)S(1)}, f32[128,8]{0,1:T(8,128)}, u32[]{:S(2)}) copy-start(f32[128,8]{0,1:T(8,128)} %param.10) | copy-start | bytes 12292
  2.3 0.7 %copy-start.1 = (f32[128]{0:T(128)S(1)}, f32[128]{0:T(128)}, u32[]{:S(2)}) copy-start(f32[128]{0:T(128)} %param.11) | copy-start | bytes 1540
  2.9 0.9 %copy-start = (bf16[128,1024]{1,0:T(8,128)(2,1)S(1)}, bf16[128,1024]{1,0:T(8,128)(2,1)}, u32[]{:S(2)}) copy-start(bf16[128,1024]{1,0:T(8,128)(2,1)} %q_ref.1) | copy-start | bytes 786436

commit v2 on v1

v2 whole, which is shorter than its diff:
```python
import functools
import math

import jax
import jax.numpy as jnp
from jax import lax
from jax.experimental import pallas as pl
from jax.experimental.pallas import tpu as pltpu
from jax.sharding import PartitionSpec as P

MESH = pl.DeviceIdType.MESH
F32 = jnp.float32
BF16 = jnp.bfloat16
NN = (((1,), (0,)), ((), ()))
NT = (((1,), (1,)), ((), ()))
LOW = -1e30
KW, VAL = 0, 1


def mm(a, b, dims=NN):
    return lax.dot_general(a, b, dims, preferred_element_type=F32)


def split(x):
    high = x.astype(BF16)
    return high, (x - high.astype(F32)).astype(BF16)


def mm3(a, b, dims=NN):
    return mm(a[0], b[0], dims) + (mm(a[0], b[1], dims) + mm(a[1], b[0], dims))


def kernel(
    chips, q_ref, k_ref, v_ref, u_ref, beta_ref, gain_ref, o_ref,
    q_own, whole, beta_own, gain_own, own_seg, sib_seg, kw, val, q_rows, peak, total, acc, chain, keys_now, far_keys,
    local, pair_send, pair_recv, line_send, line_recv, near_send, near_recv, cross_send, cross_recv, ready,
):
    half, tokens = k_ref.shape
    width = 2 * half
    heads = q_ref.shape[1] // width
    factor = math.log2(math.e) / math.sqrt(width)
    s, h = lax.axis_index("seq"), lax.axis_index("head")
    z, c = lax.div(s, 2), lax.rem(s, 2)
    last = chips - 1

    def chip(place):
        return (place * 2 + c, h)

    partner = (s, h + 1 - 2 * lax.rem(h, 2))
    sibling = (s + 1 - 2 * c, h)

    parity = lax.rem(h, 2)
    own_rows = pl.ds(parity * half, half)
    halves = (u_ref, k_ref, v_ref)
    loads = [
        pltpu.make_async_copy(src, dst, local.at[i])
        for i, (src, dst) in enumerate(
            [(src, whole.at[i, own_rows]) for i, src in enumerate(halves)]
            + [(beta_ref, beta_own), (gain_ref, gain_own), (q_ref, q_own)]
        )
    ]
    for copy in loads:
        copy.start()

    barrier = pltpu.get_barrier_semaphore()

    def tell(sem, device):
        pl.semaphore_signal(sem, inc=1, device_id=device, device_id_type=MESH)

    tell(barrier, partner)
    tell(barrier, sibling)
    pl.when(z + 1 <= last)(lambda: tell(barrier, chip(z + 1)))
    pl.when(z + 2 <= last)(lambda: tell(barrier, chip(z + 2)))
    pl.when(z <= 1)(lambda: tell(barrier, chip(last)))
    pl.when(z == 0)(lambda: tell(barrier, chip(last - 1)))
    extra = jnp.where(z == last, 2, jnp.where(z == last - 1, 1, 0))
    pl.semaphore_wait(barrier, 2 + jnp.minimum(z, 2) + extra)
    pl.when(z >= 1)(lambda: tell(ready.at[0], chip(z - 1)))
    pl.when(z >= 2)(lambda: tell(ready.at[1], chip(z - 2)))
    pl.when(z == last)(lambda: tell(ready.at[2], chip(0)))
    pl.when(z == last)(lambda: tell(ready.at[3], chip(1)))
    pl.when(z == last - 1)(lambda: tell(ready.at[3], chip(0)))

    swaps = [
        pltpu.make_async_remote_copy(
            src, whole.at[i, own_rows], pair_send.at[i], pair_recv.at[i],
            device_id=partner, device_id_type=MESH,
        )
        for i, src in enumerate(halves)
    ]
    for copy in swaps:
        copy.start()

    rows_i = lax.broadcasted_iota(jnp.int32, (tokens, tokens), 0)
    cols_i = lax.broadcasted_iota(jnp.int32, (tokens, tokens), 1)
    eye = (rows_i == cols_i).astype(F32)

    def swapped(i):
        rows = pl.ds((1 - parity) * half, half)
        loads[i].wait()
        pltpu.make_async_remote_copy(
            halves[i], whole.at[i, rows], pair_send.at[i], pair_recv.at[i],
            device_id=partner, device_id_type=MESH,
        ).wait_recv()
        return whole[i]

    buffers = (kw, val)

    def line_copy(kind, source_slot, target_slot, device):
        return pltpu.make_async_remote_copy(
            buffers[kind].at[source_slot, c],
            buffers[kind].at[target_slot, c],
            line_send.at[kind, target_slot],
            line_recv.at[kind, target_slot],
            device_id=device,
            device_id_type=MESH,
        )

    def near_copy(kind, slot):
        return pltpu.make_async_remote_copy(
            buffers[kind].at[slot, c],
            buffers[kind].at[slot, c],
            near_send.at[kind, slot],
            near_recv.at[kind, slot],
            device_id=sibling,
            device_id_type=MESH,
        )

    def near_arrival(kind, slot):
        return pltpu.make_async_remote_copy(
            buffers[kind].at[slot, 1 - c],
            buffers[kind].at[slot, 1 - c],
            near_send.at[kind, slot],
            near_recv.at[kind, slot],
            device_id=sibling,
            device_id_type=MESH,
        )

    def cross_copy(kind, slot):
        return pltpu.make_async_remote_copy(
            buffers[kind].at[slot, c],
            buffers[kind].at[slot, c],
            cross_send.at[kind, slot],
            cross_recv.at[kind, slot],
            device_id=partner,
            device_id_type=MESH,
        )

    reach = chips // 2
    far = chips - reach - 1
    farthest = far - 1 + parity

    def push_forward(kind, m, act):
        goal = 2 * m + 2 - parity
        if isinstance(m, int) and m == 0:
            fits, source, place = z + goal <= last, 0, z + goal
        else:
            fits = (z >= goal - 2) & (z + 2 <= last) & (goal <= reach)
            source, place = goal - 2, z + 2

        @pl.when(fits)
        def _():
            act(line_copy(kind, source, goal, chip(place)))

    def passing(e):
        return (z + e >= chips) | (z + e < farthest)

    def push_backward(kind, m, act):
        goal = 2 * m + 2 - parity
        if isinstance(m, int) and m == 0:
            fits, source, place = z < farthest, 0, z + chips - goal
        else:
            fits = passing(goal - 2) & (goal <= farthest)
            source, place = chips + 2 - goal, z + chips - 2

        @pl.when(fits)
        def _():
            act(line_copy(kind, source, chips - goal, chip(lax.rem(place, chips))))

    def begin(copy):
        copy.start()

    def arrive(kind, slot):
        line_copy(kind, slot, slot, sibling).wait_recv()

    def spread(kind, slot):
        cross_copy(kind, slot).start()
        near_copy(kind, slot).start()

    def line_stage(kind, m):
        d = 2 * m + 2 - parity
        pl.when(z >= d)(lambda: arrive(kind, d))
        push_forward(kind, m + 1, begin)
        pl.when(z >= d)(lambda: spread(kind, d))
        inside = d <= farthest
        pl.when(inside & passing(d))(lambda: arrive(kind, chips - d))
        push_backward(kind, m + 1, begin)
        pl.when(inside & (z + d >= chips))(lambda: spread(kind, chips - d))

    def cross_stage(kind, m):
        d = 2 * m + 1 + parity

        def take(slot):
            cross_copy(kind, slot).wait_recv()
            near_copy(kind, slot).start()

        pl.when(z >= d)(lambda: take(d))
        pl.when((d <= far - parity) & (z + d >= chips))(lambda: take(chips - d))

    def clear(slot):
        kw[pl.ds(slot, 1)] = jnp.zeros((1,) + kw.shape[1:], BF16)
        val[pl.ds(slot, 1)] = jnp.zeros((1,) + val.shape[1:], BF16)

    pl.when((lax.rem(z, 2) == 1) & (z < reach))(lambda: clear(z + 1))

    @pl.when(z > reach)
    def _():
        @pl.loop(z + 1, chips)
        def _(slot):
            clear(slot)

    loads[3].wait()
    lane = lax.broadcasted_iota(jnp.int32, beta_ref.shape, 0)
    beta = jnp.sum(jnp.where(lane == lax.div(h, 2), beta_own[...], 0.0), axis=0, keepdims=True)
    raw_t = swapped(0).astype(F32)
    unit_t = raw_t * lax.rsqrt(jnp.sum(raw_t * raw_t, axis=0, keepdims=True) + 1e-06)
    scaled_t = beta * unit_t
    unit2, scaled_t2 = split(jnp.transpose(unit_t)), split(scaled_t)
    upper = cols_i > rows_i
    nil_t = jnp.where(upper, mm3(unit2, scaled_t2), 0.0)
    keys_t = swapped(1)
    keys_wide = jnp.transpose(keys_t.astype(F32))
    keys_own = keys_wide.astype(BF16)
    reach_t = jnp.where(upper, mm(keys_own, scaled_t2[0]) + mm(keys_own, scaled_t2[1]), 0.0)
    val[0, pl.ds(c, 1)] = jnp.transpose(swapped(2).astype(F32)).astype(BF16)[None]
    near_copy(VAL, 0).start()

    pl.when(z + 1 <= last)(lambda: pl.semaphore_wait(ready.at[0], 1))
    pl.when(z + 2 <= last)(lambda: pl.semaphore_wait(ready.at[1], 1))
    push_forward(VAL, 0, begin)

    inverse = eye
    size = 1
    while size < tokens:
        bits = size.bit_length() - 1
        block_r, block_c = rows_i >> bits, cols_i >> bits
        corner = jnp.where(((block_c & 1) == 1) & (block_r == block_c - 1), nil_t, 0.0)
        if size == 1:
            inverse = eye - corner
        else:
            inv2 = split(inverse)
            inverse = inverse - mm3(split(mm3(inv2, split(corner))), inv2)
        size *= 2
    solved2 = split(mm3(split(jnp.concatenate([scaled_t, reach_t], axis=0)), split(inverse)))
    ends = jnp.concatenate([eye, keys_wide], axis=0) - mm3(solved2, unit2)
    own_seg[...] = ends.astype(BF16)

    seg_swap = pltpu.make_async_remote_copy(
        own_seg, sib_seg, pair_send.at[3], pair_recv.at[3], device_id=sibling, device_id_type=MESH
    )
    seg_swap.start()
    seg_swap.wait_recv()
    first = c == 0
    own_hop, own_keys = own_seg[0:width, :], own_seg[width : width + tokens, :]
    sib_hop, sib_keys = sib_seg[0:width, :], sib_seg[width : width + tokens, :]
    moved = jnp.where(first, mm(own_keys, sib_hop), own_keys.astype(F32))
    hops = jnp.where(first, mm(own_hop, sib_hop), mm(sib_hop, own_hop))
    hops = jnp.where(first, hops[0:half, :], hops[half:, :])
    kw[0, pl.ds(c, 1)] = jnp.concatenate([moved, hops], axis=0).astype(BF16)[None]
    push_forward(KW, 0, begin)

    pl.when(z <= 1)(lambda: pl.semaphore_wait(ready.at[3], 1))
    pl.when(z == 0)(lambda: pl.semaphore_wait(ready.at[2], 1))
    push_backward(VAL, 0, begin)
    push_backward(KW, 0, begin)

    line_stage(VAL, 0)

    loads[5].wait()
    for head in range(heads):
        q_rows[head * tokens : (head + 1) * tokens, :] = q_own[:, head * width : (head + 1) * width]
    values_own = val[0, pl.ds(c, 1)].reshape(tokens, width)
    unit_t2 = split(unit_t)
    q = q_rows[...]
    products = mm(q, jnp.concatenate([unit_t2[0], unit_t2[1], keys_t], axis=1))
    causal = jnp.concatenate([rows_i >= cols_i] * heads, axis=0)
    onto = products[:, 0:tokens] + products[:, tokens : 2 * tokens]
    taken = mm3(split(jnp.where(causal, onto, 0.0)), solved2, NT)
    q_rows[...] = (q.astype(F32) - taken[:, 0:width]).astype(BF16)
    scores = (products[:, 2 * tokens :] - taken[:, width:]) * factor
    scores = jnp.where(causal, scores, LOW)
    top = jnp.max(scores, axis=1, keepdims=True)
    weights = jnp.exp2(scores - top)
    peak[...] = jnp.broadcast_to(top, peak.shape)
    total[...] = weights
    acc[...] = mm(weights.astype(BF16), values_own)

    def absorb(key_block, value_block, mask):
        scores = mask(mm(q_rows[...], key_block(), NT))
        old = peak[...]
        top = jnp.maximum(old, jnp.max(scores, axis=1, keepdims=True))
        fade = jnp.exp2(old - top)
        peak[...] = top
        parts = []
        sums = total[...] * fade
        for i in range(scores.shape[1] // width):
            weights = jnp.exp2(scores[:, i * width : (i + 1) * width] - top)
            sums = sums + weights
            parts.append(weights.astype(BF16))
        total[...] = sums
        both = jnp.concatenate(parts, axis=1) if len(parts) > 1 else parts[0]
        acc[...] = acc[...] * fade + mm(both, value_block())

    near_arrival(VAL, 0).wait_recv()

    @pl.when(c == 1)
    def _():
        keys_now[0:tokens, :] = (sib_seg[width : width + tokens, :].astype(F32) * factor).astype(BF16)
        absorb(lambda: keys_now[0:tokens, :], lambda: val[0, 0], lambda x: x)

    chain[...] = jnp.where(first, eye, sib_seg[0:width, :].astype(F32)).astype(BF16)

    def hop_of(d):
        return jnp.concatenate(
            [kw[d, 0, tokens : tokens + half, :], kw[d, 1, tokens : tokens + half, :]], axis=0
        )

    def await_block(d):
        for kind in (KW, VAL):
            near_arrival(kind, d).wait_recv()

    @pl.loop(0, reach // 2 + 1)
    def _(i):
        m = i - 1

        @pl.when(2 * i < reach)
        def _():
            line_stage(KW, i)

        @pl.when(2 * i + 2 < reach)
        def _():
            line_stage(VAL, i + 1)

        @pl.when(i >= 1)
        def _():
            cross_stage(KW, m)
            cross_stage(VAL, m)

        @pl.when((i >= 1) & (z >= 2 * m + 1))
        def _():
            d1, d2 = 2 * m + 1, 2 * m + 2
            await_block(d1)
            pl.when(z >= d2)(lambda: await_block(d2))
            for j, d in enumerate((d1, d2)):
                now = chain[...]
                for core in range(2):
                    block = mm(kw[d, core, 0:tokens, :], now) * factor
                    at = (2 * j + core) * tokens
                    keys_now[at : at + tokens, :] = block.astype(BF16)
                chain[...] = mm(hop_of(d), now).astype(BF16)
            both = z >= d2

            def mask(scores):
                n = 2 * tokens
                return jnp.concatenate([scores[:, 0:n], jnp.where(both, scores[:, n:], LOW)], axis=1)

            absorb(
                lambda: keys_now[...],
                lambda: val[pl.ds(d1, 2)].reshape(4 * tokens, width),
                mask,
            )

    nearest, block = reach + 1, 2 * tokens

    @pl.when(z >= nearest)
    def _():
        for d in range(nearest, chips):
            pl.when(z >= d)(lambda d=d: await_block(d))
        so_far = None
        for d in range(nearest + 1, chips):
            at = (d - nearest) * block
            if so_far is None:
                for core in range(2):
                    far_keys[at + core * tokens : at + (core + 1) * tokens, :] = kw[d, core, 0:tokens, :]
                so_far = hop_of(d)
            else:
                for core in range(2):
                    far_keys[at + core * tokens : at + (core + 1) * tokens, :] = mm(
                        kw[d, core, 0:tokens, :], so_far
                    ).astype(BF16)
                so_far = mm(hop_of(d), so_far).astype(BF16)
        now = chain[...]
        for core in range(2):
            far_keys[core * tokens : (core + 1) * tokens, :] = (
                mm(kw[nearest, core, 0:tokens, :], now) * factor
            ).astype(BF16)
        beyond = mm(hop_of(nearest), now).astype(BF16)
        far_keys[block:, :] = (mm(far_keys[block:, :], beyond) * factor).astype(BF16)

        def mask(scores):
            return jnp.concatenate(
                [
                    jnp.where(z >= nearest + i, scores[:, i * block : (i + 1) * block], LOW)
                    for i in range(chips - nearest)
                ],
                axis=1,
            )

        absorb(
            lambda: far_keys[...],
            lambda: val[nearest:chips].reshape((chips - nearest) * block, width),
            mask,
        )

    loads[4].wait()
    gain = gain_own[...]
    for head in range(heads):
        span = slice(head * tokens, (head + 1) * tokens)
        mixed = acc[span, :] / jnp.sum(total[span, :], axis=1, keepdims=True)
        strength = lax.rsqrt(jnp.mean(mixed * mixed, axis=1, keepdims=True) + 1e-06)
        o_ref[:, head * width : (head + 1) * width] = (mixed * strength * gain).astype(BF16)

    def left(copy):
        copy.wait_send()

    for copy in swaps:
        copy.wait_send()
    seg_swap.wait_send()
    near_copy(VAL, 0).wait_send()

    for kind in (KW, VAL):
        push_forward(kind, 0, left)
        push_backward(kind, 0, left)

        @pl.loop(1, reach // 2)
        def _(m, kind=kind):
            push_forward(kind, m, left)
            push_backward(kind, m, left)

        @pl.loop(1, chips)
        def _(d, kind=kind):
            @pl.when(z >= d)
            def _():
                near_copy(kind, d).wait_send()
                pl.when(lax.rem(d, 2) == parity)(lambda: cross_copy(kind, d).wait_send())


def solution(mesh):
    chips = mesh.shape["seq"] // 2

    def step(q, k, v, u, beta, gain):
        tokens, width = k.shape[0], 2 * k.shape[1]
        rows = tokens * (q.shape[1] // width)
        slots = chips + 1
        piece = tokens + width // 2
        return pl.pallas_call(
            functools.partial(kernel, chips),
            out_shape=jax.ShapeDtypeStruct(q.shape, BF16),
            in_specs=[pl.BlockSpec(memory_space=pltpu.HBM)] * 6,
            out_specs=pl.BlockSpec(memory_space=pltpu.VMEM),
            scratch_shapes=[
                pltpu.VMEM(q.shape, BF16),
                pltpu.VMEM((3, width, tokens), BF16),
                pltpu.VMEM((beta.shape[1], tokens), F32),
                pltpu.VMEM((1, width), F32),
                pltpu.VMEM((width + tokens, width), BF16),
                pltpu.VMEM((width + tokens, width), BF16),
                pltpu.VMEM((slots, 2, piece, width), BF16),
                pltpu.VMEM((slots, 2, tokens, width), BF16),
                pltpu.VMEM((rows, width), BF16),
                pltpu.VMEM((rows, width), F32),
                pltpu.VMEM((rows, width), F32),
                pltpu.VMEM((rows, width), F32),
                pltpu.VMEM((width, width), BF16),
                pltpu.VMEM((4 * tokens, width), BF16),
                pltpu.VMEM(((chips - chips // 2 - 1) * 2 * tokens, width), BF16),
                pltpu.SemaphoreType.DMA((6,)),
                pltpu.SemaphoreType.DMA((4,)),
                pltpu.SemaphoreType.DMA((4,)),
                pltpu.SemaphoreType.DMA((2, slots)),
                pltpu.SemaphoreType.DMA((2, slots)),
                pltpu.SemaphoreType.DMA((2, slots)),
                pltpu.SemaphoreType.DMA((2, slots)),
                pltpu.SemaphoreType.DMA((2, slots)),
                pltpu.SemaphoreType.DMA((2, slots)),
                pltpu.SemaphoreType.REGULAR((4,)),
            ],
            compiler_params=pltpu.CompilerParams(
                collective_id=0, has_side_effects=True, vmem_limit_bytes=60 * 2**20
            ),
        )(q, k.T, v.T, u.T, beta.T, gain.reshape(1, width))

    return jax.shard_map(
        step,
        mesh=mesh,
        in_specs=(P("seq", "head"),) * 4 + (P("seq", None), P()),
        out_specs=P("seq", "head"),
        check_vma=False,
    )
```

time: 54.7 us -> 43.9 us (0.80)
  the two profiles are of different devices: /device:TPU:485 before, /device:TPU:421 now
where the time goes in v2:
time: 43.9 us; the launch traced here: 43.7 us
  Pallas kernels  42.1 us (96%)
  local copies, waits for them, and re-layouts  1.67 us (4%)
    pallas_call x1, Pallas kernels, step(): pl.pallas_call(functools.partial(kernel, chips), out_shape=jax.ShapeDtype...  42.1 us
    unnamed x1, local copies, waits for them, and re-layouts  1.67 us

profile of v2, /device:TPU:421, one launch (start us, length us, event | category | flops | bytes accessed | tf_op | source)
XLA Modules:
  0.0 43.7 jit_solution(15452806548258183308)
XLA Ops:
  0.0 42.1 %shard_map.64 = bf16[128,1024]{1,0:T(8,128)(2,1)} custom-call(bf16[128,1024]{1,0:T(8,128)(2,1)} %q_ref.1, bf16[64,128]{1,0:T(8,128)(2,1)} %bitcast.5, bf16[64,128]{1,0:T(8,128)(2,1)} %bitcast.6, bf16[64,128]{1,0:T(8,128)(2,1)} %bitcast.7, f32[8,128]{1,0:T(8,128)} %bitcast.8, f32[1,128]{1,0:T(1,128)} %bitcast.9), custom_call_target="tpu_custom_call" | custom-call | tf_op jit(solution)/shard_map/pallas_call | solution.py:456
  42.1 1.7 %copy.8 = bf16[128,1024]{1,0:T(8,128)(2,1)} copy(bf16[128,1024]{1,0:T(8,128)(2,1)} %shard_map.64) | data formatting | bytes 524288

commit v3 on v2

--- a/solution.py
+++ b/solution.py
@@ -14,7 +14,7 @@
 NN = (((1,), (0,)), ((), ()))
 NT = (((1,), (1,)), ((), ()))
 LOW = -1e30
-KW, VAL = 0, 1
+KEY, VAL = 0, 1
 
 
 def mm(a, b, dims=NN):
@@ -32,7 +32,7 @@
 
 def kernel(
     chips, q_ref, k_ref, v_ref, u_ref, beta_ref, gain_ref, o_ref,
-    q_own, whole, beta_own, gain_own, own_seg, sib_seg, kw, val, q_rows, peak, total, acc, chain, keys_now, far_keys,
+    q_own, whole, beta_own, gain_own, own_seg, sib_seg, key, val, q_rows, peak, total, acc, chain, keys_now, far_keys,
     local, pair_send, pair_recv, line_send, line_recv, near_send, near_recv, cross_send, cross_recv, ready,
 ):
     half, tokens = k_ref.shape
@@ -104,42 +104,43 @@
         ).wait_recv()
         return whole[i]
 
-    buffers = (kw, val)
+    buffers = (key, val)
 
     def line_copy(kind, source_slot, target_slot, device):
         return pltpu.make_async_remote_copy(
-            buffers[kind].at[source_slot, c],
-            buffers[kind].at[target_slot, c],
+            buffers[kind].at[source_slot, c, parity],
+            buffers[kind].at[target_slot, c, parity],
             line_send.at[kind, target_slot],
             line_recv.at[kind, target_slot],
             device_id=device,
             device_id_type=MESH,
         )
 
-    def near_copy(kind, slot):
+    part = tokens // 2
+
+    def near_piece(kind, slot, core):
+        return buffers[kind].at[slot, core]
+
+    def near_transfer(kind, slot, core):
         return pltpu.make_async_remote_copy(
-            buffers[kind].at[slot, c],
-            buffers[kind].at[slot, c],
+            near_piece(kind, slot, core),
+            near_piece(kind, slot, core),
             near_send.at[kind, slot],
             near_recv.at[kind, slot],
             device_id=sibling,
             device_id_type=MESH,
         )
 
+    def near_copy(kind, slot):
+        return near_transfer(kind, slot, c)
+
     def near_arrival(kind, slot):
+        return near_transfer(kind, slot, 1 - c)
+
+    def cross_copy(kind, slot, side):
         return pltpu.make_async_remote_copy(
-            buffers[kind].at[slot, 1 - c],
-            buffers[kind].at[slot, 1 - c],
-            near_send.at[kind, slot],
-            near_recv.at[kind, slot],
-            device_id=sibling,
-            device_id_type=MESH,
-        )
-
-    def cross_copy(kind, slot):
-        return pltpu.make_async_remote_copy(
-            buffers[kind].at[slot, c],
-            buffers[kind].at[slot, c],
+            buffers[kind].at[slot, c, side],
+            buffers[kind].at[slot, c, side],
             cross_send.at[kind, slot],
             cross_recv.at[kind, slot],
             device_id=partner,
@@ -148,34 +149,28 @@
 
     reach = chips // 2
     far = chips - reach - 1
-    farthest = far - 1 + parity
-
-    def push_forward(kind, m, act):
-        goal = 2 * m + 2 - parity
-        if isinstance(m, int) and m == 0:
-            fits, source, place = z + goal <= last, 0, z + goal
-        else:
-            fits = (z >= goal - 2) & (z + 2 <= last) & (goal <= reach)
-            source, place = goal - 2, z + 2
-
-        @pl.when(fits)
-        def _():
-            act(line_copy(kind, source, goal, chip(place)))
-
-    def passing(e):
-        return (z + e >= chips) | (z + e < farthest)
-
-    def push_backward(kind, m, act):
-        goal = 2 * m + 2 - parity
-        if isinstance(m, int) and m == 0:
-            fits, source, place = z < farthest, 0, z + chips - goal
-        else:
-            fits = passing(goal - 2) & (goal <= farthest)
-            source, place = chips + 2 - goal, z + chips - 2
-
-        @pl.when(fits)
-        def _():
-            act(line_copy(kind, source, chips - goal, chip(lax.rem(place, chips))))
+
+    def forward_relays(kind, d, act):
+        @pl.when((z >= d) & (d + 1 <= reach) & (z + 1 <= last))
+        def _():
+            act(line_copy(kind, d, d + 1, chip(z + 1)))
+
+        @pl.when((z >= d) & (d + 2 <= reach) & (z + 2 <= last))
+        def _():
+            act(line_copy(kind, d, d + 2, chip(z + 2)))
+
+    def backward_relays(kind, e, act):
+        slot = lax.rem(chips - e, chips)
+        wrapped = z + e >= chips
+        held = (z + e < far) | wrapped
+
+        @pl.when(held & (wrapped | (z == 0)) & (e + 1 <= far))
+        def _():
+            act(line_copy(kind, slot, chips - e - 1, chip(lax.rem(z + chips - 1, chips))))
+
+        @pl.when(held & (e + 2 < far))
+        def _():
+            act(line_copy(kind, slot, chips - e - 2, chip(lax.rem(z + chips - 2, chips))))
 
     def begin(copy):
         copy.start()
@@ -184,36 +179,55 @@
         line_copy(kind, slot, slot, sibling).wait_recv()
 
     def spread(kind, slot):
-        cross_copy(kind, slot).start()
-        near_copy(kind, slot).start()
+        cross_copy(kind, slot, parity).start()
 
     def line_stage(kind, m):
-        d = 2 * m + 2 - parity
-        pl.when(z >= d)(lambda: arrive(kind, d))
-        push_forward(kind, m + 1, begin)
-        pl.when(z >= d)(lambda: spread(kind, d))
-        inside = d <= farthest
-        pl.when(inside & passing(d))(lambda: arrive(kind, chips - d))
-        push_backward(kind, m + 1, begin)
-        pl.when(inside & (z + d >= chips))(lambda: spread(kind, chips - d))
+        d1, d2 = 2 * m + 1, 2 * m + 2
+        pl.when(z >= d2)(lambda: arrive(kind, d2))
+        forward_relays(kind, d2, begin)
+        pl.when(z >= d2)(lambda: spread(kind, d2))
+
+        @pl.when(z >= d1)
+        def _():
+            arrive(kind, d1)
+            spread(kind, d1)
+
+        @pl.when((d2 < far) & ((z + d2 < far) | (z + d2 >= chips)))
+        def _():
+            arrive(kind, chips - d2)
+
+        @pl.when(d2 < far)
+        def _():
+            backward_relays(kind, d2, begin)
+
+        @pl.when((d2 < far) & (z + d2 >= chips))
+        def _():
+            spread(kind, chips - d2)
+
+        @pl.when((d1 <= far) & (z + d1 >= chips))
+        def _():
+            arrive(kind, chips - d1)
+            spread(kind, chips - d1)
 
     def cross_stage(kind, m):
-        d = 2 * m + 1 + parity
+        d1, d2 = 2 * m + 1, 2 * m + 2
 
         def take(slot):
-            cross_copy(kind, slot).wait_recv()
+            cross_copy(kind, slot, 1 - parity).wait_recv()
             near_copy(kind, slot).start()
 
-        pl.when(z >= d)(lambda: take(d))
-        pl.when((d <= far - parity) & (z + d >= chips))(lambda: take(chips - d))
+        pl.when(z >= d1)(lambda: take(d1))
+        pl.when(z >= d2)(lambda: take(d2))
+        pl.when((d2 < far) & (z + d2 >= chips))(lambda: take(chips - d2))
+        pl.when((d1 <= far) & (z + d1 >= chips))(lambda: take(chips - d1))
 
     def clear(slot):
-        kw[pl.ds(slot, 1)] = jnp.zeros((1,) + kw.shape[1:], BF16)
-        val[pl.ds(slot, 1)] = jnp.zeros((1,) + val.shape[1:], BF16)
-
-    pl.when((lax.rem(z, 2) == 1) & (z < reach))(lambda: clear(z + 1))
-
-    @pl.when(z > reach)
+        for buffer in buffers:
+            buffer[pl.ds(slot, 1)] = jnp.zeros((1,) + buffer.shape[1:], BF16)
+
+    pl.when((lax.rem(z, 2) == 1) & (z < reach - 1))(lambda: clear(z + 1))
+
+    @pl.when(z >= reach - 1)
     def _():
         @pl.loop(z + 1, chips)
         def _(slot):
@@ -232,12 +246,13 @@
     keys_wide = jnp.transpose(keys_t.astype(F32))
     keys_own = keys_wide.astype(BF16)
     reach_t = jnp.where(upper, mm(keys_own, scaled_t2[0]) + mm(keys_own, scaled_t2[1]), 0.0)
-    val[0, pl.ds(c, 1)] = jnp.transpose(swapped(2).astype(F32)).astype(BF16)[None]
+    values_own = jnp.transpose(swapped(2).astype(F32)).astype(BF16)
+    val[0, pl.ds(c, 1)] = values_own.reshape((1,) + val.shape[2:])
     near_copy(VAL, 0).start()
 
     pl.when(z + 1 <= last)(lambda: pl.semaphore_wait(ready.at[0], 1))
     pl.when(z + 2 <= last)(lambda: pl.semaphore_wait(ready.at[1], 1))
-    push_forward(VAL, 0, begin)
+    forward_relays(VAL, 0, begin)
 
     inverse = eye
     size = 1
@@ -266,20 +281,22 @@
     moved = jnp.where(first, mm(own_keys, sib_hop), own_keys.astype(F32))
     hops = jnp.where(first, mm(own_hop, sib_hop), mm(sib_hop, own_hop))
     hops = jnp.where(first, hops[0:half, :], hops[half:, :])
-    kw[0, pl.ds(c, 1)] = jnp.concatenate([moved, hops], axis=0).astype(BF16)[None]
-    push_forward(KW, 0, begin)
+    quarter = half // 2
+    for side in range(2):
+        own_part = jnp.concatenate([moved[side * part : (side + 1) * part, :], hops[side * quarter : (side + 1) * quarter, :]], axis=0)
+        key[0, pl.ds(c, 1), side] = own_part.astype(BF16)[None]
+    forward_relays(KEY, 0, begin)
 
     pl.when(z <= 1)(lambda: pl.semaphore_wait(ready.at[3], 1))
     pl.when(z == 0)(lambda: pl.semaphore_wait(ready.at[2], 1))
-    push_backward(VAL, 0, begin)
-    push_backward(KW, 0, begin)
+    backward_relays(VAL, 0, begin)
+    backward_relays(KEY, 0, begin)
 
     line_stage(VAL, 0)
 
     loads[5].wait()
     for head in range(heads):
         q_rows[head * tokens : (head + 1) * tokens, :] = q_own[:, head * width : (head + 1) * width]
-    values_own = val[0, pl.ds(c, 1)].reshape(tokens, width)
     unit_t2 = split(unit_t)
     q = q_rows[...]
     products = mm(q, jnp.concatenate([unit_t2[0], unit_t2[1], keys_t], axis=1))
@@ -316,26 +333,43 @@
     @pl.when(c == 1)
     def _():
         keys_now[0:tokens, :] = (sib_seg[width : width + tokens, :].astype(F32) * factor).astype(BF16)
-        absorb(lambda: keys_now[0:tokens, :], lambda: val[0, 0], lambda x: x)
+        absorb(lambda: keys_now[0:tokens, :], lambda: val[0, 0].reshape(tokens, width), lambda x: x)
 
     chain[...] = jnp.where(first, eye, sib_seg[0:width, :].astype(F32)).astype(BF16)
 
+    block = 2 * tokens
+
     def hop_of(d):
-        return jnp.concatenate(
-            [kw[d, 0, tokens : tokens + half, :], kw[d, 1, tokens : tokens + half, :]], axis=0
-        )
-
-    def await_block(d):
-        for kind in (KW, VAL):
+        return key[d, :, :, part:, :].reshape(width, width)
+
+    def keys_of(d):
+        return key[d, :, :, 0:part, :].reshape(block, width)
+
+    def carry(j, d):
+        now = chain[...]
+        keys_now[j * block : (j + 1) * block, :] = (mm(keys_of(d), now) * factor).astype(BF16)
+        chain[...] = mm(hop_of(d), now).astype(BF16)
+
+    def await_block(d, kinds=(KEY, VAL)):
+        for kind in kinds:
             near_arrival(kind, d).wait_recv()
 
-    @pl.loop(0, reach // 2 + 1)
+    def masked(first_block):
+        def mask(scores):
+            return jnp.concatenate(
+                [
+                    jnp.where(z >= first_block + j, scores[:, j * block : (j + 1) * block], LOW)
+                    for j in range(scores.shape[1] // block)
+                ],
+                axis=1,
+            )
+
+        return mask
+
+    @pl.loop(0, reach // 2)
     def _(i):
         m = i - 1
-
-        @pl.when(2 * i < reach)
-        def _():
-            line_stage(KW, i)
+        line_stage(KEY, i)
 
         @pl.when(2 * i + 2 < reach)
         def _():
@@ -343,7 +377,7 @@
 
         @pl.when(i >= 1)
         def _():
-            cross_stage(KW, m)
+            cross_stage(KEY, m)
             cross_stage(VAL, m)
 
         @pl.when((i >= 1) & (z >= 2 * m + 1))
@@ -351,65 +385,52 @@
             d1, d2 = 2 * m + 1, 2 * m + 2
             await_block(d1)
             pl.when(z >= d2)(lambda: await_block(d2))
-            for j, d in enumerate((d1, d2)):
-                now = chain[...]
-                for core in range(2):
-                    block = mm(kw[d, core, 0:tokens, :], now) * factor
-                    at = (2 * j + core) * tokens
-                    keys_now[at : at + tokens, :] = block.astype(BF16)
-                chain[...] = mm(hop_of(d), now).astype(BF16)
-            both = z >= d2
-
-            def mask(scores):
-                n = 2 * tokens
-                return jnp.concatenate([scores[:, 0:n], jnp.where(both, scores[:, n:], LOW)], axis=1)
-
+            carry(0, d1)
+            carry(1, d2)
             absorb(
-                lambda: keys_now[...],
-                lambda: val[pl.ds(d1, 2)].reshape(4 * tokens, width),
-                mask,
+                lambda: keys_now[0 : 2 * block, :],
+                lambda: val[pl.ds(d1, 2)].reshape(2 * block, width),
+                masked(d1),
             )
 
-    nearest, block = reach + 1, 2 * tokens
-
-    @pl.when(z >= nearest)
+    tail, beyond = reach - 1, reach + 2
+
+    @pl.when(z >= beyond)
     def _():
-        for d in range(nearest, chips):
+        for d in range(beyond, chips):
             pl.when(z >= d)(lambda d=d: await_block(d))
         so_far = None
-        for d in range(nearest + 1, chips):
-            at = (d - nearest) * block
+        for d in range(beyond, chips):
+            at = (d - beyond) * block
             if so_far is None:
-                for core in range(2):
-                    far_keys[at + core * tokens : at + (core + 1) * tokens, :] = kw[d, core, 0:tokens, :]
+                far_keys[at : at + block, :] = keys_of(d)
                 so_far = hop_of(d)
             else:
-                for core in range(2):
-                    far_keys[at + core * tokens : at + (core + 1) * tokens, :] = mm(
-                        kw[d, core, 0:tokens, :], so_far
-                    ).astype(BF16)
+                far_keys[at : at + block, :] = mm(keys_of(d), so_far).astype(BF16)
                 so_far = mm(hop_of(d), so_far).astype(BF16)
-        now = chain[...]
-        for core in range(2):
-            far_keys[core * tokens : (core + 1) * tokens, :] = (
-                mm(kw[nearest, core, 0:tokens, :], now) * factor
-            ).astype(BF16)
-        beyond = mm(hop_of(nearest), now).astype(BF16)
-        far_keys[block:, :] = (mm(far_keys[block:, :], beyond) * factor).astype(BF16)
-
-        def mask(scores):
-            return jnp.concatenate(
-                [
-                    jnp.where(z >= nearest + i, scores[:, i * block : (i + 1) * block], LOW)
-                    for i in range(chips - nearest)
-                ],
-                axis=1,
-            )
-
+
+    cross_stage(KEY, reach // 2 - 1)
+    cross_stage(VAL, reach // 2 - 1)
+
+    @pl.when(z >= tail)
+    def _():
+        for d in (tail, tail + 1, tail + 2):
+            pl.when(z >= d)(lambda d=d: await_block(d))
+        for j, d in enumerate((tail, tail + 1, tail + 2)):
+            carry(j, d)
+        absorb(
+            lambda: keys_now[...],
+            lambda: val[tail : tail + 3].reshape(3 * block, width),
+            masked(tail),
+        )
+
+    @pl.when(z >= beyond)
+    def _():
+        far_keys[...] = (mm(far_keys[...], chain[...]) * factor).astype(BF16)
         absorb(
             lambda: far_keys[...],
-            lambda: val[nearest:chips].reshape((chips - nearest) * block, width),
-            mask,
+            lambda: val[beyond:chips].reshape((chips - beyond) * block, width),
+            masked(beyond),
         )
 
     loads[4].wait()
@@ -428,21 +449,21 @@
     seg_swap.wait_send()
     near_copy(VAL, 0).wait_send()
 
-    for kind in (KW, VAL):
-        push_forward(kind, 0, left)
-        push_backward(kind, 0, left)
-
-        @pl.loop(1, reach // 2)
+    for kind in (KEY, VAL):
+
+        @pl.loop(0, reach // 2)
         def _(m, kind=kind):
-            push_forward(kind, m, left)
-            push_backward(kind, m, left)
-
-        @pl.loop(1, chips)
-        def _(d, kind=kind):
-            @pl.when(z >= d)
-            def _():
+            forward_relays(kind, 2 * m, left)
+            backward_relays(kind, 2 * m, left)
+
+    @pl.loop(1, chips)
+    def _(d):
+        @pl.when(z >= d)
+        def _():
+            for kind in (KEY, VAL):
                 near_copy(kind, d).wait_send()
-                pl.when(lax.rem(d, 2) == parity)(lambda: cross_copy(kind, d).wait_send())
+            for kind in (KEY, VAL):
+                cross_copy(kind, d, parity).wait_send()
 
 
 def solution(mesh):
@@ -452,7 +473,6 @@
         tokens, width = k.shape[0], 2 * k.shape[1]
         rows = tokens * (q.shape[1] // width)
         slots = chips + 1
-        piece = tokens + width // 2
         return pl.pallas_call(
             functools.partial(kernel, chips),
             out_shape=jax.ShapeDtypeStruct(q.shape, BF16),
@@ -465,15 +485,15 @@
                 pltpu.VMEM((1, width), F32),
                 pltpu.VMEM((width + tokens, width), BF16),
                 pltpu.VMEM((width + tokens, width), BF16),
-                pltpu.VMEM((slots, 2, piece, width), BF16),
-                pltpu.VMEM((slots, 2, tokens, width), BF16),
+                pltpu.VMEM((slots, 2, 2, tokens // 2 + width // 4, width), BF16),
+                pltpu.VMEM((slots, 2, 2, tokens // 2, width), BF16),
                 pltpu.VMEM((rows, width), BF16),
                 pltpu.VMEM((rows, width), F32),
                 pltpu.VMEM((rows, width), F32),
                 pltpu.VMEM((rows, width), F32),
                 pltpu.VMEM((width, width), BF16),
-                pltpu.VMEM((4 * tokens, width), BF16),
-                pltpu.VMEM(((chips - chips // 2 - 1) * 2 * tokens, width), BF16),
+                pltpu.VMEM((6 * tokens, width), BF16),
+                pltpu.VMEM(((chips - chips // 2 - 2) * 2 * tokens, width), BF16),
                 pltpu.SemaphoreType.DMA((6,)),
                 pltpu.SemaphoreType.DMA((4,)),
                 pltpu.SemaphoreType.DMA((4,)),

time: 43.9 us -> 41.5 us (0.945)
  the two profiles are of different devices: /device:TPU:421 before, /device:TPU:435 now
where the time goes in v3:
time: 41.5 us; the launch traced here: 41.3 us
  Pallas kernels  39.6 us (95%)
  local copies, waits for them, and re-layouts  1.67 us (4%)
    pallas_call x1, Pallas kernels, step(): pl.pallas_call(functools.partial(kernel, chips), out_shape=jax.ShapeDtype...  39.6 us
    unnamed x1, local copies, waits for them, and re-layouts  1.67 us

profile of v3, /device:TPU:435, one launch (start us, length us, event | category | flops | bytes accessed | tf_op | source)
XLA Modules:
  0.0 41.3 jit_solution(17961731788553019419)
XLA Ops:
  0.0 39.6 %shard_map.64 = bf16[128,1024]{1,0:T(8,128)(2,1)} custom-call(bf16[128,1024]{1,0:T(8,128)(2,1)} %q_ref.1, bf16[64,128]{1,0:T(8,128)(2,1)} %bitcast.5, bf16[64,128]{1,0:T(8,128)(2,1)} %bitcast.6, bf16[64,128]{1,0:T(8,128)(2,1)} %bitcast.7, f32[8,128]{1,0:T(8,128)} %bitcast.8, f32[1,128]{1,0:T(1,128)} %bitcast.9), custom_call_target="tpu_custom_call" | custom-call | tf_op jit(solution)/shard_map/pallas_call | solution.py:476
  39.7 1.7 %copy.8 = bf16[128,1024]{1,0:T(8,128)(2,1)} copy(bf16[128,1024]{1,0:T(8,128)(2,1)} %shard_map.64) | data formatting | bytes 524288

commit v4 on v3

--- a/solution.py
+++ b/solution.py
@@ -371,14 +371,14 @@
         m = i - 1
         line_stage(KEY, i)
 
-        @pl.when(2 * i + 2 < reach)
-        def _():
-            line_stage(VAL, i + 1)
-
         @pl.when(i >= 1)
         def _():
             cross_stage(KEY, m)
             cross_stage(VAL, m)
+
+        @pl.when(2 * i + 2 < reach)
+        def _():
+            line_stage(VAL, i + 1)
 
         @pl.when((i >= 1) & (z >= 2 * m + 1))
         def _():

time: 41.5 us -> 40.8 us (0.983)
  Pallas kernels: 39.6 us -> 38.9 us
    pallas_call x1, Pallas kernels: 39.6 us -> 38.9 us  [step(): pl.pallas_call(functools.partial(kernel, chips), out_shape=jax.ShapeDtype...]
where the time goes in v4:
time: 40.8 us; the launch traced here: 40.6 us
  Pallas kernels  38.9 us (95%)
  local copies, waits for them, and re-layouts  1.67 us (4%)
    pallas_call x1, Pallas kernels, step(): pl.pallas_call(functools.partial(kernel, chips), out_shape=jax.ShapeDtype...  38.9 us
    unnamed x1, local copies, waits for them, and re-layouts  1.67 us

profile of v4, /device:TPU:435, one launch (start us, length us, event | category | flops | bytes accessed | tf_op | source)
XLA Modules:
  0.0 40.6 jit_solution(15353049896716229868)
XLA Ops:
  0.0 38.9 %shard_map.64 = bf16[128,1024]{1,0:T(8,128)(2,1)} custom-call(bf16[128,1024]{1,0:T(8,128)(2,1)} %q_ref.1, bf16[64,128]{1,0:T(8,128)(2,1)} %bitcast.5, bf16[64,128]{1,0:T(8,128)(2,1)} %bitcast.6, bf16[64,128]{1,0:T(8,128)(2,1)} %bitcast.7, f32[8,128]{1,0:T(8,128)} %bitcast.8, f32[1,128]{1,0:T(1,128)} %bitcast.9), custom_call_target="tpu_custom_call" | custom-call | tf_op jit(solution)/shard_map/pallas_call | solution.py:476
  38.9 1.7 %copy.8 = bf16[128,1024]{1,0:T(8,128)(2,1)} copy(bf16[128,1024]{1,0:T(8,128)(2,1)} %shard_map.64) | data formatting | bytes 524288

commit v5 on v4

--- a/solution.py
+++ b/solution.py
@@ -32,7 +32,7 @@
 
 def kernel(
     chips, q_ref, k_ref, v_ref, u_ref, beta_ref, gain_ref, o_ref,
-    q_own, whole, beta_own, gain_own, own_seg, sib_seg, key, val, q_rows, peak, total, acc, chain, keys_now, far_keys,
+    q_own, whole, beta_own, gain_own, own_seg, sib_seg, key, val, q_rows, peak, total, acc, chain, keys_now,
     local, pair_send, pair_recv, line_send, line_recv, near_send, near_recv, cross_send, cross_recv, ready,
 ):
     half, tokens = k_ref.shape
@@ -401,12 +401,12 @@
             pl.when(z >= d)(lambda d=d: await_block(d))
         so_far = None
         for d in range(beyond, chips):
-            at = (d - beyond) * block
+            at = (d - tail) * block
             if so_far is None:
-                far_keys[at : at + block, :] = keys_of(d)
+                keys_now[at : at + block, :] = keys_of(d)
                 so_far = hop_of(d)
             else:
-                far_keys[at : at + block, :] = mm(keys_of(d), so_far).astype(BF16)
+                keys_now[at : at + block, :] = mm(keys_of(d), so_far).astype(BF16)
                 so_far = mm(hop_of(d), so_far).astype(BF16)
 
     cross_stage(KEY, reach // 2 - 1)
@@ -418,26 +418,26 @@
             pl.when(z >= d)(lambda d=d: await_block(d))
         for j, d in enumerate((tail, tail + 1, tail + 2)):
             carry(j, d)
+
+    def absorb_rest(count):
         absorb(
-            lambda: keys_now[...],
-            lambda: val[tail : tail + 3].reshape(3 * block, width),
+            lambda: keys_now[0 : count * block, :],
+            lambda: val[tail : tail + count].reshape(count * block, width),
             masked(tail),
         )
 
+    pl.when((z >= tail) & (z < beyond))(lambda: absorb_rest(3))
+
     @pl.when(z >= beyond)
     def _():
-        far_keys[...] = (mm(far_keys[...], chain[...]) * factor).astype(BF16)
-        absorb(
-            lambda: far_keys[...],
-            lambda: val[beyond:chips].reshape((chips - beyond) * block, width),
-            masked(beyond),
-        )
+        keys_now[3 * block :, :] = (mm(keys_now[3 * block :, :], chain[...]) * factor).astype(BF16)
+        absorb_rest(chips - tail)
 
     loads[4].wait()
     gain = gain_own[...]
     for head in range(heads):
         span = slice(head * tokens, (head + 1) * tokens)
-        mixed = acc[span, :] / jnp.sum(total[span, :], axis=1, keepdims=True)
+        mixed = acc[span, :] * (1.0 / jnp.sum(total[span, :], axis=1, keepdims=True))
         strength = lax.rsqrt(jnp.mean(mixed * mixed, axis=1, keepdims=True) + 1e-06)
         o_ref[:, head * width : (head + 1) * width] = (mixed * strength * gain).astype(BF16)
 
@@ -492,8 +492,7 @@
                 pltpu.VMEM((rows, width), F32),
                 pltpu.VMEM((rows, width), F32),
                 pltpu.VMEM((width, width), BF16),
-                pltpu.VMEM((6 * tokens, width), BF16),
-                pltpu.VMEM(((chips - chips // 2 - 2) * 2 * tokens, width), BF16),
+                pltpu.VMEM(((chips - chips // 2 + 1) * 2 * tokens, width), BF16),
                 pltpu.SemaphoreType.DMA((6,)),
                 pltpu.SemaphoreType.DMA((4,)),
                 pltpu.SemaphoreType.DMA((4,)),

time: 40.8 us -> 40.2 us (0.985)
  the two profiles are of different devices: /device:TPU:435 before, /device:TPU:439 now
where the time goes in v5:
time: 40.2 us; the launch traced here: 40 us
  Pallas kernels  38.4 us (96%)
  local copies, waits for them, and re-layouts  1.67 us (4%)
    pallas_call x1, Pallas kernels, step(): pl.pallas_call(functools.partial(kernel, chips), out_shape=jax.ShapeDtype...  38.4 us
    unnamed x1, local copies, waits for them, and re-layouts  1.67 us

profile of v5, /device:TPU:439, one launch (start us, length us, event | category | flops | bytes accessed | tf_op | source)
XLA Modules:
  0.0 40.0 jit_solution(14100369924419774768)
XLA Ops:
  0.0 38.4 %shard_map.64 = bf16[128,1024]{1,0:T(8,128)(2,1)} custom-call(bf16[128,1024]{1,0:T(8,128)(2,1)} %q_ref.1, bf16[64,128]{1,0:T(8,128)(2,1)} %bitcast.5, bf16[64,128]{1,0:T(8,128)(2,1)} %bitcast.6, bf16[64,128]{1,0:T(8,128)(2,1)} %bitcast.7, f32[8,128]{1,0:T(8,128)} %bitcast.8, f32[1,128]{1,0:T(1,128)} %bitcast.9), custom_call_target="tpu_custom_call" | custom-call | tf_op jit(solution)/shard_map/pallas_call | solution.py:476
  38.4 1.7 %copy.8 = bf16[128,1024]{1,0:T(8,128)(2,1)} copy(bf16[128,1024]{1,0:T(8,128)(2,1)} %shard_map.64) | data formatting | bytes 524288
